TPU v7x, 32 devices: a whole 2x2x4 slice. The times are simulated.
32 devices in a mesh: dp: 16 (over z, y, core), head: 2 (over x).
Axes of the slice: x: 2, y: 2, z: 4, core: 2. Of those that a mesh axis runs over, the one named last changes fastest.
Arguments:
- media_tokens: bfloat16 [256, 256, 1024], P('dp'), may hold values from -6 to 6
- latents: bfloat16 [256, 64, 1024], P('dp'), may hold values from -6 to 6
- cotangent: bfloat16 [256, 64, 1024], P('dp'), may hold values from -6 to 6
- image_counts: int32 [128], P('dp'), may hold values from 1 to 2, as said below
- media_gain: float32 [1024], replicated, may hold values from 0.1 to 1.9
- media_bias: float32 [1024], replicated, may hold values from -3 to 3
- latent_gain: float32 [1024], replicated, may hold values from 0.1 to 1.9
- latent_bias: float32 [1024], replicated, may hold values from -3 to 3
- ff_gain: float32 [1024], replicated, may hold values from 0.1 to 1.9
- ff_bias: float32 [1024], replicated, may hold values from -3 to 3
- w_query: bfloat16 [1024, 512], P('dp', 'head'), may hold values from -0.1875 to 0.1875
- w_keyval: bfloat16 [1024, 2, 512], P('dp', None, 'head'), may hold values from -0.1875 to 0.1875
- w_attn_out: bfloat16 [512, 1024], P('head', 'dp'), may hold values from -1 to 1
- w_up: bfloat16 [1024, 4096], P('dp', 'head'), may hold values from -0.1875 to 0.1875
- w_down: bfloat16 [4096, 1024], P('head', 'dp'), may hold values from -0.09375 to 0.09375
Outputs:
- latents_out: float32 [256, 64, 1024], P('dp', 'head')
- media_grad: float32 [256, 256, 1024], P('dp', 'head')
- latent_grad: float32 [256, 64, 1024], P('dp', 'head')
- grad_query: float32 [1024, 512], P('dp', 'head')
- grad_keyval: float32 [1024, 2, 512], P('dp', None, 'head')
- grad_attn_out: float32 [512, 1024], P('head', 'dp')
- grad_up: float32 [1024, 4096], P('dp', 'head')
- grad_down: float32 [4096, 1024], P('head', 'dp')
- norm_grads: float32 [6, 1024], replicated
Inputs may be any that keep to these rules, and one draw needn't show every extreme that they name: `image_counts`: samples are stored in order, 8 to each index of dp. The images of a dp index's samples fill its 16 slots from slot 0 on, sample after sample; the other slots of that index are empty. In every draw some sample has 2 images and some dp index has all its slots filled.
All inputs are finite; a program needn't handle non-finite values.
Results may differ from a plain program's by a relative error of at most 0.019.
Values may be sent and summed in bfloat16 or wider, within the bound.
No kernel may reach another device: no remote copies, remote signals or barrier semaphores. Data moves between devices by JAX's collectives and lax.ppermute only.
A program may use at most 192 MiB of HBM per device.

v0:
```python
import math
import jax
import jax.numpy as jnp
from jax import lax
from jax.sharding import PartitionSpec as P

HD = 64


def layer_norm(values, gain, bias):
    centre = values - jnp.mean(values, axis=-1, keepdims=True)
    spread = jnp.mean(centre * centre, axis=-1, keepdims=True)
    return centre * lax.rsqrt(spread + 1e-05) * gain + bias


def norm_back(values, gain, bias, grad):
    result, pull = jax.vjp(layer_norm, values, gain, bias)
    return pull(grad)


def gelu_exact(values):
    return jax.nn.gelu(values, approximate=False)


def row_share(values, count):
    start = lax.axis_index("head") * count
    return lax.dynamic_slice_in_dim(values, start, count, 1)


def local(
    media_tokens,
    latents,
    cotangent,
    image_counts,
    media_gain,
    media_bias,
    latent_gain,
    latent_bias,
    ff_gain,
    ff_bias,
    w_query,
    w_keyval,
    w_attn_out,
    w_up,
    w_down,
):
    images, patches = (media_tokens.shape[0], media_tokens.shape[1])
    lat_rows = latents.shape[1]
    head_count = w_query.shape[1] // HD
    head_groups = lax.axis_size("head")
    patch_share = patches // head_groups
    lat_share = lat_rows // head_groups
    score_scale = 1.0 / math.sqrt(HD)
    live_mask = (jnp.arange(images, dtype=jnp.int32) < jnp.sum(image_counts)).astype(jnp.float32)[
        :, None, None
    ]
    query_all, keyval_all, up_all = (
        lax.all_gather(w_query, "dp", axis=0, tiled=True),
        lax.all_gather(w_keyval, "dp", axis=0, tiled=True),
        lax.all_gather(w_up, "dp", axis=0, tiled=True),
    )
    attn_all, down_all = (
        lax.all_gather(w_attn_out, "dp", axis=1, tiled=True),
        lax.all_gather(w_down, "dp", axis=1, tiled=True),
    )
    media_full = media_tokens.astype(jnp.float32)
    latent_full = latents.astype(jnp.float32)
    normed_media = layer_norm(media_full, media_gain, media_bias).astype(jnp.bfloat16)
    normed_lat = layer_norm(latent_full, latent_gain, latent_bias).astype(jnp.bfloat16)
    sources = jnp.concatenate([normed_media, normed_lat], axis=1)
    src_rows = sources.shape[1]
    query_act = jnp.einsum(
        "ild,dc->ilc", normed_lat, query_all, preferred_element_type=jnp.float32
    ).astype(jnp.bfloat16)
    keyval = jnp.einsum(
        "ird,dkc->ikrc", sources, keyval_all, preferred_element_type=jnp.float32
    ).astype(jnp.bfloat16)
    query_blocks = query_act.reshape(images, lat_rows, head_count, HD)
    key_blocks = keyval[:, 0].reshape(images, src_rows, head_count, HD)
    value_blocks = keyval[:, 1].reshape(images, src_rows, head_count, HD)
    scores = (
        jnp.einsum("ilhe,irhe->ihlr", query_blocks, key_blocks, preferred_element_type=jnp.float32)
        * score_scale
    )
    row_top = jnp.max(scores, axis=-1, keepdims=True)
    exp_terms = jnp.exp(scores - row_top)
    row_total = jnp.sum(exp_terms, axis=-1, keepdims=True)
    probs_low = (exp_terms / row_total).astype(jnp.bfloat16)
    log_total = row_top + jnp.log(row_total)
    mixed_heads = (
        jnp.einsum("ihlr,irhe->ilhe", probs_low, value_blocks, preferred_element_type=jnp.float32)
        .astype(jnp.bfloat16)
        .reshape(images, lat_rows, head_count * HD)
    )
    attn_part = jnp.einsum("ilc,cd->ild", mixed_heads, attn_all, preferred_element_type=jnp.float32)
    middle = latent_full + lax.psum(attn_part.astype(jnp.bfloat16), "head").astype(jnp.float32)
    normed_mid = layer_norm(middle, ff_gain, ff_bias).astype(jnp.bfloat16)
    up_act = jnp.einsum("ild,df->ilf", normed_mid, up_all, preferred_element_type=jnp.float32)
    hidden, gelu_pull = jax.vjp(gelu_exact, up_act)
    hidden_low = hidden.astype(jnp.bfloat16)
    ff_part = jnp.einsum("ilf,fd->ild", hidden_low, down_all, preferred_element_type=jnp.float32)
    final_lat = middle + lax.psum(ff_part.astype(jnp.bfloat16), "head").astype(jnp.float32)
    latent_rows_share = row_share(latent_full, lat_share)
    latents_out = jnp.where(live_mask > 0, row_share(final_lat, lat_share), latent_rows_share)
    grad_final = cotangent.astype(jnp.float32) * live_mask
    final_low = grad_final.astype(jnp.bfloat16)
    grad_down = jnp.einsum("ilf,ild->fd", hidden_low, final_low, preferred_element_type=jnp.float32)
    grad_hidden = jnp.einsum("ild,fd->ilf", final_low, down_all, preferred_element_type=jnp.float32)
    up_low = gelu_pull(grad_hidden)[0].astype(jnp.bfloat16)
    grad_up = jnp.einsum("ild,ilf->df", normed_mid, up_low, preferred_element_type=jnp.float32)
    mid_part = jnp.einsum("ilf,df->ild", up_low, up_all, preferred_element_type=jnp.float32)
    grad_normed_mid = lax.psum(mid_part.astype(jnp.bfloat16), "head").astype(jnp.float32)
    mid_back, ff_gain_grad, ff_bias_grad = norm_back(middle, ff_gain, ff_bias, grad_normed_mid)
    grad_mid = grad_final + mid_back
    mid_low = grad_mid.astype(jnp.bfloat16)
    grad_attn = jnp.einsum("ilc,ild->cd", mixed_heads, mid_low, preferred_element_type=jnp.float32)
    grad_mixed = (
        jnp.einsum("ild,cd->ilc", mid_low, attn_all, preferred_element_type=jnp.float32)
        .astype(jnp.bfloat16)
        .reshape(images, lat_rows, head_count, HD)
    )
    scores_again = (
        jnp.einsum("ilhe,irhe->ihlr", query_blocks, key_blocks, preferred_element_type=jnp.float32)
        * score_scale
    )
    attn_probs = jnp.exp(scores_again - log_total)
    grad_values = jnp.einsum(
        "ihlr,ilhe->irhe", probs_low, grad_mixed, preferred_element_type=jnp.float32
    ).astype(jnp.bfloat16)
    grad_probs = jnp.einsum(
        "ilhe,irhe->ihlr", grad_mixed, value_blocks, preferred_element_type=jnp.float32
    )
    grad_scores = (
        attn_probs * (grad_probs - jnp.sum(attn_probs * grad_probs, axis=-1, keepdims=True))
    ).astype(jnp.bfloat16)
    grad_query_act = (
        (
            jnp.einsum(
                "ihlr,irhe->ilhe", grad_scores, key_blocks, preferred_element_type=jnp.float32
            )
            * score_scale
        )
        .astype(jnp.bfloat16)
        .reshape(images, lat_rows, head_count * HD)
    )
    grad_keys = (
        jnp.einsum("ihlr,ilhe->irhe", grad_scores, query_blocks, preferred_element_type=jnp.float32)
        * score_scale
    ).astype(jnp.bfloat16)
    grad_keyval_act = jnp.stack(
        [
            grad_keys.reshape(images, src_rows, head_count * HD),
            grad_values.reshape(images, src_rows, head_count * HD),
        ],
        axis=1,
    )
    grad_query = jnp.einsum(
        "ild,ilc->dc", normed_lat, grad_query_act, preferred_element_type=jnp.float32
    )
    grad_keyval = jnp.einsum(
        "ird,ikrc->dkc", sources, grad_keyval_act, preferred_element_type=jnp.float32
    )
    lat_part = jnp.einsum(
        "ikrc,dkc->ird",
        grad_keyval_act[:, :, patches:],
        keyval_all,
        preferred_element_type=jnp.float32,
    )
    lat_part = lat_part + jnp.einsum(
        "ilc,dc->ild", grad_query_act, query_all, preferred_element_type=jnp.float32
    )
    media_part = jnp.einsum(
        "ikrc,dkc->ird",
        grad_keyval_act[:, :, :patches],
        keyval_all,
        preferred_element_type=jnp.float32,
    )
    grad_normed_media, grad_normed_lat = (
        lax.psum_scatter(
            media_part.astype(jnp.bfloat16), "head", scatter_dimension=1, tiled=True
        ).astype(jnp.float32),
        lax.psum_scatter(
            lat_part.astype(jnp.bfloat16), "head", scatter_dimension=1, tiled=True
        ).astype(jnp.float32),
    )
    media_share = row_share(media_full, patch_share)
    media_grad, media_gain_grad, media_bias_grad = norm_back(
        media_share, media_gain, media_bias, grad_normed_media
    )
    lat_back, lat_gain_grad, lat_bias_grad = norm_back(
        latent_rows_share, latent_gain, latent_bias, grad_normed_lat
    )
    cot_share = row_share(cotangent.astype(jnp.float32), lat_share)
    latent_grad = jnp.where(live_mask > 0, row_share(grad_mid, lat_share) + lat_back, cot_share)
    gain_terms = jnp.stack(
        [
            media_gain_grad,
            media_bias_grad,
            lat_gain_grad,
            lat_bias_grad,
            ff_gain_grad / head_groups,
            ff_bias_grad / head_groups,
        ]
    )
    norm_grads = lax.psum(gain_terms, ("dp", "head"))
    grad_query, grad_keyval, grad_up = (
        lax.psum_scatter(
            grad_query.astype(jnp.bfloat16), "dp", scatter_dimension=0, tiled=True
        ).astype(jnp.float32),
        lax.psum_scatter(
            grad_keyval.astype(jnp.bfloat16), "dp", scatter_dimension=0, tiled=True
        ).astype(jnp.float32),
        lax.psum_scatter(
            grad_up.astype(jnp.bfloat16), "dp", scatter_dimension=0, tiled=True
        ).astype(jnp.float32),
    )
    grad_attn, grad_down = (
        lax.psum_scatter(
            grad_attn.astype(jnp.bfloat16), "dp", scatter_dimension=1, tiled=True
        ).astype(jnp.float32),
        lax.psum_scatter(
            grad_down.astype(jnp.bfloat16), "dp", scatter_dimension=1, tiled=True
        ).astype(jnp.float32),
    )
    return (
        latents_out,
        media_grad,
        latent_grad,
        grad_query,
        grad_keyval,
        grad_attn,
        grad_up,
        grad_down,
        norm_grads,
    )


def solution(mesh):
    return jax.shard_map(
        local,
        mesh=mesh,
        in_specs=(
            P("dp", None, None),
            P("dp", None, None),
            P("dp", None, None),
            P("dp"),
            P(),
            P(),
            P(),
            P(),
            P(),
            P(),
            P("dp", "head"),
            P("dp", None, "head"),
            P("head", "dp"),
            P("dp", "head"),
            P("head", "dp"),
        ),
        out_specs=(
            P("dp", "head", None),
            P("dp", "head", None),
            P("dp", "head", None),
            P("dp", "head"),
            P("dp", None, "head"),
            P("head", "dp"),
            P("dp", "head"),
            P("head", "dp"),
            P(),
        ),
        check_vma=False,
    )
```

profile of v0, /device:TPU:0, one launch (start us, length us, event | category | flops | bytes accessed | tf_op | source)
XLA Modules:
  0.0 992.0 jit_solution(9586764897184007495)
XLA Ops:
  13.0 4.7 convert_reduce_fusion.1
  18.8 2.8 multiply_reduce_fusion
  21.6 25.3 %all_gather.16 = bf16[1024,256]{1,0:T(8,128)(2,1)S(1)} all-gather(bf16[64,256]{1,0:T(8,128)(2,1)S(1)} %copy-done.29), channel_id=1, replica_groups=mesh['dp'=16,'head'=2] {'dp'}, dimensions={0}, use_global_device_ids=true | all-gather | bytes 557056 | tf_op jit(solution)/shard_map/all_gather | solution.py:58
  52.2 20.8 %all_gather.17 = bf16[256,1024]{0,1:T(8,128)(2,1)} all-gather(bf16[256,64]{0,1:T(8,128)(2,1)S(1)} %copy-done.30), channel_id=1, replica_groups=mesh['dp'=16,'head'=2] {'dp'}, dimensions={1}, use_global_device_ids=true | all-gather | bytes 557056 | tf_op jit(solution)/shard_map/all_gather | solution.py:63
  73.0 8.6 add_convert_fusion
  81.6 8.6 convert_bitcast_fusion
  92.9 4.5 copy.43
  97.4 3.1 multiply_reduce_fusion.3
  104.8 4.5 copy.42
  109.3 4.1 convolution_convert_fusion.2
  119.9 59.0 %all-reduce.4.cloned.1.call-done = bf16[16,64,1024]{2,1,0:T(8,128)(2,1)} async-done(((bf16[16,64,1024]{2,1,0:T(8,128)(2,1)}), bf16[16,64,1024]{2,1,0:T(8,128)(2,1)}) %all-reduce.4.cloned.1.call-update) | async-done | bytes 2097168 | tf_op jit(solution)/shard_map/psum | solution.py:96
  182.2 49.7 %all-gather.6.cloned.1.call-done = bf16[1024,2048]{1,0:T(8,128)(2,1)} async-done(((bf16[64,2048]{1,0:T(8,128)(2,1)}), bf16[1024,2048]{1,0:T(8,128)(2,1)}) %all-gather.6.cloned.1.call-update) | async-done | bytes 4194320 | tf_op jit(solution)/shard_map/all_gather | solution.py:60
  231.9 9.4 fusion.28
  241.3 3.2 copy-done.11
  244.5 19.8 %multiply_convert_fusion = (bf16[16,64,2048]{2,1,0:T(8,128)(2,1)}, f32[16,64,2048]{2,1,0:T(8,128)}) fusion(f32[16,64,2048]{2,1,0:T(8,128)S(1)} %get-tuple-element.59, u16[64,2048]{1,0:T(8,128)(2,1)S(1)} %get-tuple-element.32, u16[64,2048]{1,0:T(8,128)(2,1)S(1)} %get-tuple-element.31), kind=kLoop, calls=%fused_computation.24 | loop fusion | flops 146800640 | bytes 21495808 | tf_op jit(solution)/shard_map/convert_element_type | solution.py:100
  264.3 18.9 %all-gather.8.cloned.1.call-done = bf16[2048,1024]{0,1:T(8,128)(2,1)} async-done(((bf16[2048,64]{0,1:T(8,128)(2,1)}), bf16[2048,1024]{0,1:T(8,128)(2,1)}) %all-gather.8.cloned.1.call-update) | async-done | bytes 4194320 | tf_op jit(solution)/shard_map/all_gather | solution.py:64
  283.2 12.8 %add_convert_fusion.1 = bf16[16,64,2048]{2,1,0:T(8,128)(2,1)S(1)} fusion(f32[16,64,2048]{2,1,0:T(8,128)} %get-tuple-element.46, f32[16,64,2048]{2,1,0:T(8,128)} %copy-done.11, bf16[2048,1024]{0,1:T(8,128)(2,1)} %all-gather.8.cloned.1.call-done, f32[16]{0:T(128)S(1)} %compare_convert_fusion, bf16[16,64,1024]{2,1,0:T(8,128)(2,1)} %param.17), kind=kOutput, calls=%fused_computation.23 | convolution fusion | flops 4327473152 | bytes 27263040 | tf_op jit(solution)/shard_map/ild,fd->ilf/dot_general | solution.py:108
  296.1 5.7 fusion.35
  301.8 5.8 fusion.38
  307.7 106.8 %all-reduce.6.cloned.1.call-done = (bf16[16,64,1024]{2,1,0:T(8,128)(2,1)}, bf16[16,64,1024]{2,1,0:T(8,128)(2,1)}) async-done(((bf16[16,64,1024]{2,1,0:T(8,128)(2,1)}, bf16[16,64,1024]{2,1,0:T(8,128)(2,1)}), (bf16[16,64,1024]{2,1,0:T(8,128)(2,1)}, bf16[16,64,1024]{2,1,0:T(8,128)(2,1)})) %all-reduce.6.cloned.1.call-update) | async-done | bytes 4194320 | tf_op jit(solution)/shard_map/psum | solution.py:112
  414.5 4.2 convert_reduce_fusion.2
  418.7 3.1 fusion.16
  421.8 3.3 add_add_fusion.2
  432.3 4.9 convolution_convert_fusion
  437.1 4.6 copy.50
  441.7 6.8 multiply_reduce_fusion.2
  454.7 4.6 copy.49
  459.5 4.2 multiply_convert_fusion.4
  466.0 10.8 %bitcast_convert_fusion.3 = bf16[1024,2,256]{2,0,1:T(8,128)(2,1)} fusion(bf16[16,1,320,256]{3,2,1,0:T(8,128)(2,1)} %copy.50, bf16[16,1,320,256]{3,2,1,0:T(8,128)(2,1)} %copy.49, bf16[16,64,1024]{2,1,0:T(8,128)(2,1)} %copy-done.19, bf16[16,256,1024]{2,1,0:T(8,128)(2,1)} %add_convert_fusion), kind=kOutput, calls=%fused_computation.96 | convolution fusion | flops 5400690688 | bytes 16777216 | tf_op jit(solution)/shard_map/ird,ikrc->dkc/dot_general | solution.py:160
  476.9 9.7 bitcast_convert_fusion.2
  486.9 9.5 bitcast_convert_fusion.1
  496.4 2.9 fusion.45
  502.3 10.5 %bitcast_convert_fusion = bf16[16,256,1024]{2,1,0:T(8,128)(2,1)} fusion(bf16[16,1,320,256]{3,2,1,0:T(8,128)(2,1)} %copy.49, bf16[16,1,320,256]{3,2,1,0:T(8,128)(2,1)} %copy.50, bf16[1024,2,256]{2,0,1:T(8,128)(2,1)} %all-gather.4.cloned.1.call-done), kind=kOutput, calls=%fused_computation | convolution fusion | flops 4301258752 | bytes 14680064 | tf_op jit(solution)/shard_map/ikrc,dkc->ird/dot_general | solution.py:172
  512.9 11.3 %convert_element_type.145 = f32[16,256,1024]{2,1,0:T(8,128)} convert(bf16[16,256,1024]{2,1,0:T(8,128)(2,1)} %param.15) | non-fusion elementwise | flops 4194304 | bytes 25165824 | tf_op jit(solution)/shard_map/convert_element_type | solution.py:66
  531.0 3.9 dynamic-slice_reduce_fusion
  537.2 37.4 %reduce-scatter.12.cloned.1.call-done = bf16[64,256]{1,0:T(8,128)(2,1)} async-done(((bf16[1024,256]{1,0:T(8,128)(2,1)}), bf16[64,256]{1,0:T(8,128)(2,1)}) %reduce-scatter.12.cloned.1.call-update) | async-done | bytes 32784 | tf_op jit(solution)/shard_map/reduce_scatter | solution.py:207
  576.0 59.2 %reduce-scatter.14.cloned.1.call-done = bf16[64,2,256]{2,0,1:T(8,128)(2,1)} async-done(((bf16[1024,2,256]{2,0,1:T(8,128)(2,1)}), bf16[64,2,256]{2,0,1:T(8,128)(2,1)}) %reduce-scatter.14.cloned.1.call-update) | async-done | bytes 65552 | tf_op jit(solution)/shard_map/reduce_scatter | solution.py:210
  636.7 74.5 %reduce-scatter.18.cloned.1.call-done = bf16[64,2048]{1,0:T(8,128)(2,1)} async-done(((bf16[1024,2048]{1,0:T(8,128)(2,1)}), bf16[64,2048]{1,0:T(8,128)(2,1)}) %reduce-scatter.18.cloned.1.call-update) | async-done | bytes 262160 | tf_op jit(solution)/shard_map/reduce_scatter | solution.py:213
  713.0 73.5 %reduce-scatter.20.cloned.1.call-done = bf16[2048,64]{0,1:T(8,128)(2,1)} async-done(((bf16[2048,1024]{0,1:T(8,128)(2,1)}), bf16[2048,64]{0,1:T(8,128)(2,1)}) %reduce-scatter.20.cloned.1.call-update) | async-done | bytes 262160 | tf_op jit(solution)/shard_map/reduce_scatter | solution.py:221
  788.2 32.0 %reduce-scatter.10.cloned.1.call-done = bf16[16,32,1024]{2,1,0:T(8,128)(2,1)} async-done(((bf16[16,64,1024]{2,1,0:T(8,128)(2,1)}), bf16[16,32,1024]{2,1,0:T(8,128)(2,1)}) %reduce-scatter.10.cloned.1.call-update) | async-done | bytes 1048592 | tf_op jit(solution)/shard_map/reduce_scatter | solution.py:182
  820.2 2.9 multiply_reduce_fusion.6
  823.2 3.1 fusion.33
  826.3 5.6 dynamic-slice_select_fusion
  831.9 90.3 %reduce-scatter.8.cloned.1.call-done = bf16[16,128,1024]{2,1,0:T(8,128)(2,1)} async-done(((bf16[16,256,1024]{2,1,0:T(8,128)(2,1)}), bf16[16,128,1024]{2,1,0:T(8,128)(2,1)}) %reduce-scatter.8.cloned.1.call-update) | async-done | bytes 4194320 | tf_op jit(solution)/shard_map/reduce_scatter | solution.py:179
  922.2 7.5 multiply_reduce_fusion.1
  929.8 6.7 fusion.4
  936.5 40.0 %psum.31 = f32[6,1024]{1,0:T(8,128)} all-reduce(f32[6,1024]{1,0:T(8,128)S(1)} %stack.25), channel_id=1, replica_groups=mesh['dp'=16,'head'=2] {'dp','head'}, use_global_device_ids=true, to_apply=%region_36.37 | all-reduce | flops 6144 | bytes 49152 | tf_op jit(solution)/shard_map/psum | solution.py:205
  976.6 8.1 broadcast_add_fusion
  (154 shorter events, 63.5 us)
Async XLA Ops:
  7.2 74.4 %all-gather.4.cloned.1.call-start = ((), (), s32[]{:S(2)}) async-start(), calls=%async_computation.7 | async-start | bytes 1114112 | tf_op jit(solution)/shard_map/all_gather | solution.py:59
  8.7 170.1 %all-reduce.4.cloned.1.call-start = ((), (), s32[]{:S(2)}) async-start(), calls=%async_computation.8 | async-start | bytes 4194304 | tf_op jit(solution)/shard_map/psum | solution.py:96
  13.0 5.8 copy-start.2
  18.8 2.9 copy-start.29
  18.8 28.1 %copy-start = (bf16[16,64,1024]{2,1,0:T(8,128)(2,1)S(1)}, bf16[16,64,1024]{2,1,0:T(8,128)(2,1)}, u32[]{:S(2)}) copy-start(bf16[16,64,1024]{2,1,0:T(8,128)(2,1)} %param.16) | copy-start | bytes 6291460
  18.8 28.1 %copy-start.24 = (f32[1024]{0:T(1024)S(1)}, f32[1024]{0:T(1024)}, u32[]{:S(2)}) copy-start(f32[1024]{0:T(1024)} %param.21) | copy-start | bytes 12292
  18.8 28.1 %copy-start.31 = (f32[1024]{0:T(1024)S(1)}, f32[1024]{0:T(1024)}, u32[]{:S(2)}) copy-start(f32[1024]{0:T(1024)} %param.22) | copy-start | bytes 12292
  46.9 5.3 copy-start.30
  46.9 26.0 %copy-start.26 = (f32[1024]{0:T(1024)S(1)}, f32[1024]{0:T(1024)}, u32[]{:S(2)}) copy-start(f32[1024]{0:T(1024)} %param.19) | copy-start | bytes 12292
  47.0 26.0 %copy-start.32 = (f32[1024]{0:T(1024)S(1)}, f32[1024]{0:T(1024)}, u32[]{:S(2)}) copy-start(f32[1024]{0:T(1024)} %param.20) | copy-start | bytes 12292
  100.5 4.3 copy-start.1
  109.3 5.1 copy-start.14
  113.4 5.2 copy-start.36
  117.1 114.8 %all-gather.6.cloned.1.call-start = ((), (), s32[]{:S(2)}) async-start(), calls=%async_computation.9 | async-start | bytes 4456448 | tf_op jit(solution)/shard_map/all_gather | solution.py:60
  117.8 165.4 %all-gather.8.cloned.1.call-start = ((), (), s32[]{:S(2)}) async-start(), calls=%async_computation.10 | async-start | bytes 4456448 | tf_op jit(solution)/shard_map/all_gather | solution.py:64
  118.4 296.1 %all-reduce.6.cloned.1.call-start = ((), (), s32[]{:S(2)}) async-start(), calls=%async_computation.18 | async-start | bytes 8388608 | tf_op jit(solution)/shard_map/psum | solution.py:112
  119.9 112.0 %copy-start.28 = (f32[1024]{0:T(1024)S(1)}, f32[1024]{0:T(1024)}, u32[]{:S(2)}) copy-start(f32[1024]{0:T(1024)} %param.23) | copy-start | bytes 12292
  119.9 112.0 %copy-start.35 = (f32[1024]{0:T(1024)S(1)}, f32[1024]{0:T(1024)}, u32[]{:S(2)}) copy-start(f32[1024]{0:T(1024)} %param.24) | copy-start | bytes 12292
  178.9 2.4 copy-start.3
  241.3 3.2 copy-start.11
  283.2 12.8 %copy-start.33 = (bf16[1024,2048]{1,0:T(8,128)(2,1)S(1)}, bf16[1024,2048]{1,0:T(8,128)(2,1)}, u32[]{:S(2)}) copy-start(bf16[1024,2048]{1,0:T(8,128)(2,1)} %all-gather.6.cloned.1.call-done) | copy-start | bytes 12582916
  296.0 5.8 copy-start.37
  296.1 5.8 copy-start.18
  296.1 5.8 copy-start.34
  307.7 228.0 %reduce-scatter.16.cloned.1.call-start = ((), (), s32[]{:S(2)}) async-start(), calls=%async_computation.15 | async-start | bytes 557056 | tf_op jit(solution)/shard_map/reduce_scatter | solution.py:218
  414.5 4.2 copy-start.4
  414.5 4.2 copy-start.9
  418.7 3.1 copy-start.12
  421.8 3.3 copy-start.15
  425.1 2.2 copy-start.8
  425.2 2.2 copy-start.17
  441.7 6.8 slice-start
  441.7 6.8 slice-start.1
  459.3 115.3 %reduce-scatter.12.cloned.1.call-start = ((), (), s32[]{:S(2)}) async-start(), calls=%async_computation.13 | async-start | bytes 557056 | tf_op jit(solution)/shard_map/reduce_scatter | solution.py:207
  459.5 4.2 copy-start.20
  465.9 169.2 %reduce-scatter.14.cloned.1.call-start = ((), (), s32[]{:S(2)}) async-start(), calls=%async_computation.14 | async-start | bytes 1114112 | tf_op jit(solution)/shard_map/reduce_scatter | solution.py:210
  476.8 234.4 %reduce-scatter.18.cloned.1.call-start = ((), (), s32[]{:S(2)}) async-start(), calls=%async_computation.16 | async-start | bytes 4456448 | tf_op jit(solution)/shard_map/reduce_scatter | solution.py:213
  486.6 299.9 %reduce-scatter.20.cloned.1.call-start = ((), (), s32[]{:S(2)}) async-start(), calls=%async_computation.17 | async-start | bytes 4456448 | tf_op jit(solution)/shard_map/reduce_scatter | solution.py:221
  496.4 323.8 %reduce-scatter.10.cloned.1.call-start = ((), (), s32[]{:S(2)}) async-start(), calls=%async_computation.12 | async-start | bytes 3145728 | tf_op jit(solution)/shard_map/reduce_scatter | solution.py:182
  496.4 2.9 copy-start.22
  502.0 420.2 %reduce-scatter.8.cloned.1.call-start = ((), (), s32[]{:S(2)}) async-start(), calls=%async_computation.11 | async-start | bytes 12582912 | tf_op jit(solution)/shard_map/reduce_scatter | solution.py:179
  524.2 2.6 copy-start.13
  531.0 289.2 %copy-start.25 = (f32[1024]{0:T(1024)S(1)}, f32[1024]{0:T(1024)}, u32[]{:S(2)}) copy-start(f32[1024]{0:T(1024)} %param.21) | copy-start | bytes 12292
  535.6 290.7 %copy-start.23 = (bf16[16,64,1024]{2,1,0:T(8,128)(2,1)S(1)}, bf16[16,64,1024]{2,1,0:T(8,128)(2,1)}, u32[]{:S(2)}) copy-start(bf16[16,64,1024]{2,1,0:T(8,128)(2,1)} %get-tuple-element.44) | copy-start | bytes 6291460
  820.2 6.1 copy-start.6
  820.2 6.1 copy-start.10
  826.3 95.9 %copy-start.27 = (f32[1024]{0:T(1024)S(1)}, f32[1024]{0:T(1024)}, u32[]{:S(2)}) copy-start(f32[1024]{0:T(1024)} %param.19) | copy-start | bytes 12292
  922.2 7.6 copy-start.5
  (4 other events, 4.9 us)
Sparse Core Ops, SparseCore 0:
  10.8 41.0 all-gather.3
  117.2 61.6 all-reduce.3
  181.3 50.5 all-gather.5
  234.1 49.0 all-gather.7
  307.8 106.6 all-reduce.5
  459.4 55.7 reduce-scatter.15
  519.8 54.7 reduce-scatter.11
  578.8 56.3 reduce-scatter.13
  639.5 71.7 reduce-scatter.17
  714.9 71.4 reduce-scatter.19
  789.4 30.7 reduce-scatter.9
  822.9 99.2 reduce-scatter.7
where the time goes:
time: 997 us; the launch traced here: 992 us
  waiting for transfers between devices  603 us (60%)
  other arithmetic  125 us (13%)
  matrix products  124 us (12%)
  blocking collectives  86.1 us (9%)
  local copies, waits for them, and re-layouts  37.1 us (4%)
  between operations  15.3 us (2%)
    psum x1, waiting for transfers between devices, local(): lax.psum(mid_part.astype(jnp.bfloat16), 'head').astype(jnp.float32)  107 us
    reduce_scatter x1, waiting for transfers between devices, local(): lax.psum_scatter(media_part.astype(jnp.bfloat16), 'head', scatter_dimensi...  90.3 us
    reduce_scatter x1, waiting for transfers between devices, local(): lax.psum_scatter(grad_up.astype(jnp.bfloat16), 'dp', scatter_dimension=0,...  74.5 us
    reduce_scatter x1, waiting for transfers between devices, local(): lax.psum_scatter(grad_down.astype(jnp.bfloat16), 'dp', scatter_dimension=...  73.5 us
    reduce_scatter x1, waiting for transfers between devices, local(): lax.psum_scatter(grad_keyval.astype(jnp.bfloat16), 'dp', scatter_dimensio...  59.2 us
    psum x1, waiting for transfers between devices, local(): lax.psum(attn_part.astype(jnp.bfloat16), 'head').astype(jnp.float32)  59 us
    all_gather x1, waiting for transfers between devices, local(): lax.all_gather(w_up, 'dp', axis=0, tiled=True)  49.7 us
    psum x1, blocking collectives, local(): norm_grads = lax.psum(gain_terms, ('dp', 'head'))  40 us
  transfers between devices with their start and end apart: 12, of which 10 were waited for; matrix products, arithmetic and copies ran while one was open for 15% of the time, Pallas kernels for 0%

commit v1 on v0

--- a/solution.py
+++ b/solution.py
@@ -202,7 +202,7 @@
             ff_bias_grad / head_groups,
         ]
     )
-    norm_grads = lax.psum(gain_terms, ("dp", "head"))
+    norm_grads = lax.psum(lax.psum(gain_terms, "head"), "dp")
     grad_query, grad_keyval, grad_up = (
         lax.psum_scatter(
             grad_query.astype(jnp.bfloat16), "dp", scatter_dimension=0, tiled=True

time: 997 us -> 1020 us (1.023)
  blocking collectives: 86.1 us -> 113 us
    psum x1 -> x2, blocking collectives: 40 us -> 67.2 us  [local(): norm_grads = lax.psum(lax.psum(gain_terms, 'head'), 'dp')]
where the time goes in v1:
time: 1020 us
  waiting for transfers between devices  603 us (59%)
  other arithmetic  125 us (12%)
  matrix products  124 us (12%)
  blocking collectives  113 us (11%)
  local copies, waits for them, and re-layouts  37.1 us (4%)
  between operations  15.3 us (2%)
    psum x1, waiting for transfers between devices, local(): lax.psum(mid_part.astype(jnp.bfloat16), 'head').astype(jnp.float32)  107 us
    reduce_scatter x1, waiting for transfers between devices, local(): lax.psum_scatter(media_part.astype(jnp.bfloat16), 'head', scatter_dimensi...  90.3 us
    reduce_scatter x1, waiting for transfers between devices, local(): lax.psum_scatter(grad_up.astype(jnp.bfloat16), 'dp', scatter_dimension=0,...  74.5 us
    reduce_scatter x1, waiting for transfers between devices, local(): lax.psum_scatter(grad_down.astype(jnp.bfloat16), 'dp', scatter_dimension=...  73.5 us
    psum x2, blocking collectives, local(): norm_grads = lax.psum(lax.psum(gain_terms, 'head'), 'dp')  67.2 us
    reduce_scatter x1, waiting for transfers between devices, local(): lax.psum_scatter(grad_keyval.astype(jnp.bfloat16), 'dp', scatter_dimensio...  59.2 us
    psum x1, waiting for transfers between devices, local(): lax.psum(attn_part.astype(jnp.bfloat16), 'head').astype(jnp.float32)  59 us
    all_gather x1, waiting for transfers between devices, local(): lax.all_gather(w_up, 'dp', axis=0, tiled=True)  49.7 us
  transfers between devices with their start and end apart: 12, of which 10 were waited for; matrix products, arithmetic and copies ran while one was open for 15% of the time, Pallas kernels for 0%

profile of v1, /device:TPU:0, one launch (start us, length us, event | category | flops | bytes accessed | tf_op | source)
XLA Modules:
  0.0 1019.2 jit_solution(5909180293752316863)
XLA Ops:
  13.0 4.7 convert_reduce_fusion.1
  21.6 25.3 %all_gather.16 = bf16[1024,256]{1,0:T(8,128)(2,1)S(1)} all-gather(bf16[64,256]{1,0:T(8,128)(2,1)S(1)} %copy-done.29), channel_id=1, replica_groups=mesh['dp'=16,'head'=2] {'dp'}, dimensions={0}, use_global_device_ids=true | all-gather | bytes 557056 | tf_op jit(solution)/shard_map/all_gather | solution.py:58
  52.2 20.8 %all_gather.17 = bf16[256,1024]{0,1:T(8,128)(2,1)} all-gather(bf16[256,64]{0,1:T(8,128)(2,1)S(1)} %copy-done.30), channel_id=1, replica_groups=mesh['dp'=16,'head'=2] {'dp'}, dimensions={1}, use_global_device_ids=true | all-gather | bytes 557056 | tf_op jit(solution)/shard_map/all_gather | solution.py:63
  73.0 8.6 add_convert_fusion
  81.6 8.6 convert_bitcast_fusion
  92.9 4.5 copy.43
  97.4 3.1 multiply_reduce_fusion.3
  104.8 4.5 copy.42
  109.3 4.1 convolution_convert_fusion.2
  119.9 59.0 %all-reduce.4.cloned.1.call-done = bf16[16,64,1024]{2,1,0:T(8,128)(2,1)} async-done(((bf16[16,64,1024]{2,1,0:T(8,128)(2,1)}), bf16[16,64,1024]{2,1,0:T(8,128)(2,1)}) %all-reduce.4.cloned.1.call-update) | async-done | bytes 2097168 | tf_op jit(solution)/shard_map/psum | solution.py:96
  182.2 49.7 %all-gather.6.cloned.1.call-done = bf16[1024,2048]{1,0:T(8,128)(2,1)} async-done(((bf16[64,2048]{1,0:T(8,128)(2,1)}), bf16[1024,2048]{1,0:T(8,128)(2,1)}) %all-gather.6.cloned.1.call-update) | async-done | bytes 4194320 | tf_op jit(solution)/shard_map/all_gather | solution.py:60
  231.9 9.4 fusion.28
  241.3 3.2 copy-done.11
  244.5 19.8 %multiply_convert_fusion = (bf16[16,64,2048]{2,1,0:T(8,128)(2,1)}, f32[16,64,2048]{2,1,0:T(8,128)}) fusion(f32[16,64,2048]{2,1,0:T(8,128)S(1)} %get-tuple-element.59, u16[64,2048]{1,0:T(8,128)(2,1)S(1)} %get-tuple-element.32, u16[64,2048]{1,0:T(8,128)(2,1)S(1)} %get-tuple-element.31), kind=kLoop, calls=%fused_computation.24 | loop fusion | flops 146800640 | bytes 21495808 | tf_op jit(solution)/shard_map/convert_element_type | solution.py:100
  264.3 18.9 %all-gather.8.cloned.1.call-done = bf16[2048,1024]{0,1:T(8,128)(2,1)} async-done(((bf16[2048,64]{0,1:T(8,128)(2,1)}), bf16[2048,1024]{0,1:T(8,128)(2,1)}) %all-gather.8.cloned.1.call-update) | async-done | bytes 4194320 | tf_op jit(solution)/shard_map/all_gather | solution.py:64
  283.2 12.8 %add_convert_fusion.1 = bf16[16,64,2048]{2,1,0:T(8,128)(2,1)S(1)} fusion(f32[16,64,2048]{2,1,0:T(8,128)} %get-tuple-element.46, f32[16,64,2048]{2,1,0:T(8,128)} %copy-done.11, bf16[2048,1024]{0,1:T(8,128)(2,1)} %all-gather.8.cloned.1.call-done, f32[16]{0:T(128)S(1)} %compare_convert_fusion, bf16[16,64,1024]{2,1,0:T(8,128)(2,1)} %param.17), kind=kOutput, calls=%fused_computation.23 | convolution fusion | flops 4327473152 | bytes 27263040 | tf_op jit(solution)/shard_map/ild,fd->ilf/dot_general | solution.py:108
  296.1 5.7 fusion.35
  301.8 5.8 fusion.38
  307.7 106.8 %all-reduce.6.cloned.1.call-done = (bf16[16,64,1024]{2,1,0:T(8,128)(2,1)}, bf16[16,64,1024]{2,1,0:T(8,128)(2,1)}) async-done(((bf16[16,64,1024]{2,1,0:T(8,128)(2,1)}, bf16[16,64,1024]{2,1,0:T(8,128)(2,1)}), (bf16[16,64,1024]{2,1,0:T(8,128)(2,1)}, bf16[16,64,1024]{2,1,0:T(8,128)(2,1)})) %all-reduce.6.cloned.1.call-update) | async-done | bytes 4194320 | tf_op jit(solution)/shard_map/psum | solution.py:112
  414.5 4.2 convert_reduce_fusion.2
  418.7 3.1 fusion.16
  421.8 3.3 add_add_fusion.2
  432.3 4.9 convolution_convert_fusion
  437.1 4.6 copy.50
  441.7 6.8 multiply_reduce_fusion.2
  454.7 4.6 copy.49
  459.5 4.2 multiply_convert_fusion.4
  466.0 10.8 %bitcast_convert_fusion.3 = bf16[1024,2,256]{2,0,1:T(8,128)(2,1)} fusion(bf16[16,1,320,256]{3,2,1,0:T(8,128)(2,1)} %copy.50, bf16[16,1,320,256]{3,2,1,0:T(8,128)(2,1)} %copy.49, bf16[16,64,1024]{2,1,0:T(8,128)(2,1)} %copy-done.19, bf16[16,256,1024]{2,1,0:T(8,128)(2,1)} %add_convert_fusion), kind=kOutput, calls=%fused_computation.96 | convolution fusion | flops 5400690688 | bytes 16777216 | tf_op jit(solution)/shard_map/ird,ikrc->dkc/dot_general | solution.py:160
  476.9 9.7 bitcast_convert_fusion.2
  486.9 9.5 bitcast_convert_fusion.1
  496.4 2.9 fusion.45
  502.3 10.5 %bitcast_convert_fusion = bf16[16,256,1024]{2,1,0:T(8,128)(2,1)} fusion(bf16[16,1,320,256]{3,2,1,0:T(8,128)(2,1)} %copy.49, bf16[16,1,320,256]{3,2,1,0:T(8,128)(2,1)} %copy.50, bf16[1024,2,256]{2,0,1:T(8,128)(2,1)} %all-gather.4.cloned.1.call-done), kind=kOutput, calls=%fused_computation | convolution fusion | flops 4301258752 | bytes 14680064 | tf_op jit(solution)/shard_map/ikrc,dkc->ird/dot_general | solution.py:172
  512.9 11.3 %convert_element_type.145 = f32[16,256,1024]{2,1,0:T(8,128)} convert(bf16[16,256,1024]{2,1,0:T(8,128)(2,1)} %param.15) | non-fusion elementwise | flops 4194304 | bytes 25165824 | tf_op jit(solution)/shard_map/convert_element_type | solution.py:66
  531.0 3.9 dynamic-slice_reduce_fusion
  537.2 37.4 %reduce-scatter.12.cloned.1.call-done = bf16[64,256]{1,0:T(8,128)(2,1)} async-done(((bf16[1024,256]{1,0:T(8,128)(2,1)}), bf16[64,256]{1,0:T(8,128)(2,1)}) %reduce-scatter.12.cloned.1.call-update) | async-done | bytes 32784 | tf_op jit(solution)/shard_map/reduce_scatter | solution.py:207
  576.0 59.2 %reduce-scatter.14.cloned.1.call-done = bf16[64,2,256]{2,0,1:T(8,128)(2,1)} async-done(((bf16[1024,2,256]{2,0,1:T(8,128)(2,1)}), bf16[64,2,256]{2,0,1:T(8,128)(2,1)}) %reduce-scatter.14.cloned.1.call-update) | async-done | bytes 65552 | tf_op jit(solution)/shard_map/reduce_scatter | solution.py:210
  636.7 74.5 %reduce-scatter.18.cloned.1.call-done = bf16[64,2048]{1,0:T(8,128)(2,1)} async-done(((bf16[1024,2048]{1,0:T(8,128)(2,1)}), bf16[64,2048]{1,0:T(8,128)(2,1)}) %reduce-scatter.18.cloned.1.call-update) | async-done | bytes 262160 | tf_op jit(solution)/shard_map/reduce_scatter | solution.py:213
  713.0 73.5 %reduce-scatter.20.cloned.1.call-done = bf16[2048,64]{0,1:T(8,128)(2,1)} async-done(((bf16[2048,1024]{0,1:T(8,128)(2,1)}), bf16[2048,64]{0,1:T(8,128)(2,1)}) %reduce-scatter.20.cloned.1.call-update) | async-done | bytes 262160 | tf_op jit(solution)/shard_map/reduce_scatter | solution.py:221
  788.2 32.0 %reduce-scatter.10.cloned.1.call-done = bf16[16,32,1024]{2,1,0:T(8,128)(2,1)} async-done(((bf16[16,64,1024]{2,1,0:T(8,128)(2,1)}), bf16[16,32,1024]{2,1,0:T(8,128)(2,1)}) %reduce-scatter.10.cloned.1.call-update) | async-done | bytes 1048592 | tf_op jit(solution)/shard_map/reduce_scatter | solution.py:182
  820.2 2.9 multiply_reduce_fusion.6
  823.2 3.1 fusion.33
  826.3 5.6 dynamic-slice_select_fusion
  831.9 90.3 %reduce-scatter.8.cloned.1.call-done = bf16[16,128,1024]{2,1,0:T(8,128)(2,1)} async-done(((bf16[16,256,1024]{2,1,0:T(8,128)(2,1)}), bf16[16,128,1024]{2,1,0:T(8,128)(2,1)}) %reduce-scatter.8.cloned.1.call-update) | async-done | bytes 4194320 | tf_op jit(solution)/shard_map/reduce_scatter | solution.py:179
  922.2 7.5 multiply_reduce_fusion.1
  929.8 6.7 fusion.4
  936.5 7.2 psum.38
  943.7 60.0 %psum.39 = f32[6,1024]{1,0:T(8,128)} all-reduce(f32[6,1024]{1,0:T(8,128)S(1)} %psum.38), channel_id=1, replica_groups=mesh['dp'=16,'head'=2] {'dp'}, use_global_device_ids=true, to_apply=%region_37.38 | all-reduce | flops 6144 | bytes 49152 | tf_op jit(solution)/shard_map/psum | solution.py:205
  1003.8 8.1 broadcast_add_fusion
  (155 shorter events, 66.4 us)
Async XLA Ops:
  7.2 74.4 %all-gather.4.cloned.1.call-start = ((), (), s32[]{:S(2)}) async-start(), calls=%async_computation.7 | async-start | bytes 1114112 | tf_op jit(solution)/shard_map/all_gather | solution.py:59
  8.7 170.1 %all-reduce.4.cloned.1.call-start = ((), (), s32[]{:S(2)}) async-start(), calls=%async_computation.8 | async-start | bytes 4194304 | tf_op jit(solution)/shard_map/psum | solution.py:96
  13.0 5.8 copy-start.2
  18.8 2.9 copy-start.29
  18.8 28.1 %copy-start = (bf16[16,64,1024]{2,1,0:T(8,128)(2,1)S(1)}, bf16[16,64,1024]{2,1,0:T(8,128)(2,1)}, u32[]{:S(2)}) copy-start(bf16[16,64,1024]{2,1,0:T(8,128)(2,1)} %param.16) | copy-start | bytes 6291460
  18.8 28.1 %copy-start.24 = (f32[1024]{0:T(1024)S(1)}, f32[1024]{0:T(1024)}, u32[]{:S(2)}) copy-start(f32[1024]{0:T(1024)} %param.21) | copy-start | bytes 12292
  18.8 28.1 %copy-start.31 = (f32[1024]{0:T(1024)S(1)}, f32[1024]{0:T(1024)}, u32[]{:S(2)}) copy-start(f32[1024]{0:T(1024)} %param.22) | copy-start | bytes 12292
  46.9 5.3 copy-start.30
  46.9 26.0 %copy-start.26 = (f32[1024]{0:T(1024)S(1)}, f32[1024]{0:T(1024)}, u32[]{:S(2)}) copy-start(f32[1024]{0:T(1024)} %param.19) | copy-start | bytes 12292
  47.0 26.0 %copy-start.32 = (f32[1024]{0:T(1024)S(1)}, f32[1024]{0:T(1024)}, u32[]{:S(2)}) copy-start(f32[1024]{0:T(1024)} %param.20) | copy-start | bytes 12292
  100.5 4.3 copy-start.1
  109.3 5.1 copy-start.14
  113.4 5.2 copy-start.36
  117.1 114.8 %all-gather.6.cloned.1.call-start = ((), (), s32[]{:S(2)}) async-start(), calls=%async_computation.9 | async-start | bytes 4456448 | tf_op jit(solution)/shard_map/all_gather | solution.py:60
  117.8 165.4 %all-gather.8.cloned.1.call-start = ((), (), s32[]{:S(2)}) async-start(), calls=%async_computation.10 | async-start | bytes 4456448 | tf_op jit(solution)/shard_map/all_gather | solution.py:64
  118.4 296.1 %all-reduce.6.cloned.1.call-start = ((), (), s32[]{:S(2)}) async-start(), calls=%async_computation.18 | async-start | bytes 8388608 | tf_op jit(solution)/shard_map/psum | solution.py:112
  119.9 112.0 %copy-start.28 = (f32[1024]{0:T(1024)S(1)}, f32[1024]{0:T(1024)}, u32[]{:S(2)}) copy-start(f32[1024]{0:T(1024)} %param.23) | copy-start | bytes 12292
  119.9 112.0 %copy-start.35 = (f32[1024]{0:T(1024)S(1)}, f32[1024]{0:T(1024)}, u32[]{:S(2)}) copy-start(f32[1024]{0:T(1024)} %param.24) | copy-start | bytes 12292
  178.9 2.4 copy-start.3
  241.3 3.2 copy-start.11
  283.2 12.8 %copy-start.33 = (bf16[1024,2048]{1,0:T(8,128)(2,1)S(1)}, bf16[1024,2048]{1,0:T(8,128)(2,1)}, u32[]{:S(2)}) copy-start(bf16[1024,2048]{1,0:T(8,128)(2,1)} %all-gather.6.cloned.1.call-done) | copy-start | bytes 12582916
  296.0 5.8 copy-start.37
  296.1 5.8 copy-start.18
  296.1 5.8 copy-start.34
  307.7 228.0 %reduce-scatter.16.cloned.1.call-start = ((), (), s32[]{:S(2)}) async-start(), calls=%async_computation.15 | async-start | bytes 557056 | tf_op jit(solution)/shard_map/reduce_scatter | solution.py:218
  414.5 4.2 copy-start.4
  414.5 4.2 copy-start.9
  418.7 3.1 copy-start.12
  421.8 3.3 copy-start.15
  425.1 2.2 copy-start.8
  425.2 2.2 copy-start.17
  441.7 6.8 slice-start
  441.7 6.8 slice-start.1
  459.3 115.3 %reduce-scatter.12.cloned.1.call-start = ((), (), s32[]{:S(2)}) async-start(), calls=%async_computation.13 | async-start | bytes 557056 | tf_op jit(solution)/shard_map/reduce_scatter | solution.py:207
  459.5 4.2 copy-start.20
  465.9 169.2 %reduce-scatter.14.cloned.1.call-start = ((), (), s32[]{:S(2)}) async-start(), calls=%async_computation.14 | async-start | bytes 1114112 | tf_op jit(solution)/shard_map/reduce_scatter | solution.py:210
  476.8 234.4 %reduce-scatter.18.cloned.1.call-start = ((), (), s32[]{:S(2)}) async-start(), calls=%async_computation.16 | async-start | bytes 4456448 | tf_op jit(solution)/shard_map/reduce_scatter | solution.py:213
  486.6 299.9 %reduce-scatter.20.cloned.1.call-start = ((), (), s32[]{:S(2)}) async-start(), calls=%async_computation.17 | async-start | bytes 4456448 | tf_op jit(solution)/shard_map/reduce_scatter | solution.py:221
  496.4 323.8 %reduce-scatter.10.cloned.1.call-start = ((), (), s32[]{:S(2)}) async-start(), calls=%async_computation.12 | async-start | bytes 3145728 | tf_op jit(solution)/shard_map/reduce_scatter | solution.py:182
  496.4 2.9 copy-start.22
  502.0 420.2 %reduce-scatter.8.cloned.1.call-start = ((), (), s32[]{:S(2)}) async-start(), calls=%async_computation.11 | async-start | bytes 12582912 | tf_op jit(solution)/shard_map/reduce_scatter | solution.py:179
  524.2 2.6 copy-start.13
  531.0 289.2 %copy-start.25 = (f32[1024]{0:T(1024)S(1)}, f32[1024]{0:T(1024)}, u32[]{:S(2)}) copy-start(f32[1024]{0:T(1024)} %param.21) | copy-start | bytes 12292
  535.6 290.7 %copy-start.23 = (bf16[16,64,1024]{2,1,0:T(8,128)(2,1)S(1)}, bf16[16,64,1024]{2,1,0:T(8,128)(2,1)}, u32[]{:S(2)}) copy-start(bf16[16,64,1024]{2,1,0:T(8,128)(2,1)} %get-tuple-element.44) | copy-start | bytes 6291460
  820.2 6.1 copy-start.6
  820.2 6.1 copy-start.10
  826.3 95.9 %copy-start.27 = (f32[1024]{0:T(1024)S(1)}, f32[1024]{0:T(1024)}, u32[]{:S(2)}) copy-start(f32[1024]{0:T(1024)} %param.19) | copy-start | bytes 12292
  922.2 7.6 copy-start.5
  (4 other events, 4.9 us)
Sparse Core Ops, SparseCore 0:
  10.8 41.0 all-gather.3
  117.2 61.6 all-reduce.3
  181.3 50.5 all-gather.5
  234.1 49.0 all-gather.7
  307.8 106.6 all-reduce.5
  459.4 55.7 reduce-scatter.15
  519.8 54.7 reduce-scatter.11
  578.8 56.3 reduce-scatter.13
  639.5 71.7 reduce-scatter.17
  714.9 71.4 reduce-scatter.19
  789.4 30.7 reduce-scatter.9
  822.9 99.2 reduce-scatter.7
